TPU v7x, 256 devices: a whole 4x4x8 slice. The times are simulated.
256 devices in a mesh: shot: 8 (over y, core), band: 32 (over x, z).
Axes of the slice: x: 4, y: 4, z: 8, core: 2. Of those that a mesh axis runs over, the one named last changes fastest.
Arguments:
- sensitivity: bfloat16 [16384, 128, 128], P(('shot', 'band')), may hold values from -0.0625 to 0.0625
- bundle_of: int32 [16384], P(('shot', 'band')), may hold values from 0 to 31
- cellblock_of: int32 [16384], P(('shot', 'band')), may hold values from 0 to 15
- state: float32 [65536, 128], P('band'), may hold values from -6 to 6
- prior_velocity: float32 [65536, 128], P('band'), may hold values from -6 to 6
- observed: float32 [256, 128], P(('shot', 'band')), may hold values from -6 to 6
- pick_weight: float32 [256, 128], P(('shot', 'band')), may hold values from 0.3 to 3
Outputs:
- new_state: float32 [65536, 128], P('band')
- weighted_residual: float32 [256, 128, 128], P(('shot', 'band'))
Inputs may be any that keep to these rules, and one draw needn't show every extreme that they name: bundle_of names a bundle of the block's own source group. cellblock_of names a cell block of the block's own depth band.
All inputs are finite; a program needn't handle non-finite values.
Results may differ from a plain program's by a relative error of at most 0.0059.
Values may be sent and summed in bfloat16 or wider, within the bound.
A program may use at most 64 MiB of HBM per device.

v0:
```python
import jax
import jax.numpy as jnp
from jax import lax
from jax.sharding import PartitionSpec as P

CBLK = 128


def block_products(sensitivity, cellblock_of, probe):
    columns = probe.reshape(-1, CBLK, probe.shape[1])[cellblock_of]
    return jnp.einsum("krc,kce->kre", sensitivity, columns, preferred_element_type=jnp.float32)


def adjoint_part(sensitivity, bundle_of, cellblock_of, resid_all, cell_blocks):
    rows = resid_all[bundle_of]
    contrib = jnp.einsum("krc,kre->kce", sensitivity, rows, preferred_element_type=jnp.float32)
    summed = jax.ops.segment_sum(contrib, cellblock_of, num_segments=cell_blocks)
    return summed.reshape(cell_blocks * CBLK, rows.shape[2])


def per_device(sensitivity, bundle_of, cellblock_of, state, prior_velocity, observed, pick_weight):
    nband = lax.axis_size("band")
    owned = observed.shape[0]
    bundles = owned * nband
    cell_blocks = state.shape[0] // CBLK

    def residual_pass(probe):
        prod = block_products(sensitivity, cellblock_of, probe)
        partial_value = jax.ops.segment_sum(prod, bundle_of, num_segments=bundles)
        pred = lax.psum_scatter(partial_value, "band", scatter_dimension=0, tiled=True)
        resid = pick_weight[:, :, None] * (pred - observed[:, :, None])
        resid_all = lax.all_gather(resid.astype(jnp.bfloat16), "band", axis=0, tiled=True)
        return (resid, adjoint_part(sensitivity, bundle_of, cellblock_of, resid_all, cell_blocks))

    probe1 = (state + 0.5 * prior_velocity).astype(jnp.bfloat16)
    res1, part1 = residual_pass(probe1)

    def summed_grad(part):
        return lax.psum(part, "shot")

    grad1 = summed_grad(part1)
    middle = state + 0.5 * (prior_velocity - 0.5 * grad1)
    probe2 = (middle + 0.5 * prior_velocity).astype(jnp.bfloat16)
    res2, part2 = residual_pass(probe2)
    grad2 = summed_grad(part2)
    new_state = state + 0.5 * (prior_velocity - 0.25 * (grad1 + grad2))
    return (new_state, res2)


def solution(mesh):
    in_specs = (
        P(("shot", "band"), None, None),
        P(("shot", "band")),
        P(("shot", "band")),
        P("band", None),
        P("band", None),
        P(("shot", "band"), None),
        P(("shot", "band"), None),
    )
    out_specs = (P("band", None), P(("shot", "band"), None, None))
    return jax.shard_map(
        per_device, mesh=mesh, in_specs=in_specs, out_specs=out_specs, check_vma=False
    )
```

profile of v0, /device:TPU:2, one launch (start us, length us, event | category | flops | bytes accessed | tf_op | source)
XLA Modules:
  0.0 845.8 jit_solution(9297075635177994917)
XLA Ops:
  7.2 0.8 compare_select_fusion.1
  8.0 1.7 add_convert_fusion.1
  9.7 2.2 gather_fusion
  11.8 5.2 convolution_bitcast_fusion.3
  17.0 5.6 copy.28
  22.6 1.6 broadcast.21.clone
  24.2 13.5 %scatter_fusion = f32[32,128,128]{2,1,0:T(8,128)} fusion(f32[32,128,128]{2,1,0:T(8,128)} %broadcast.21.clone, s32[64]{0:T(128)S(1)} %copy-done.3, f32[64,128,128]{2,1,0:T(8,128)} %copy.28), kind=kCustom, calls=%fused_computation.4 | custom fusion | flops 1048576 | bytes 12583168 | tf_op jit(solution)/shard_map/scatter-add | solution.py:29
  37.8 218.6 %reduce-scatter.3.cloned.1.call-done = f32[1,128,128]{2,1,0:T(8,128)} async-done(((f32[32,128,128]{2,1,0:T(8,128)}), f32[1,128,128]{2,1,0:T(8,128)}) %reduce-scatter.3.cloned.1.call-update) | async-done | bytes 65552 | tf_op jit(solution)/shard_map/reduce_scatter | solution.py:30
  256.4 1.6 multiply_convert_fusion
  258.0 76.1 %all-gather.3.cloned.1.call-done = bf16[32,128,128]{2,1,0:T(8,128)(2,1)} async-done(((bf16[1,128,128]{2,1,0:T(8,128)(2,1)}), bf16[32,128,128]{2,1,0:T(8,128)(2,1)}) %all-gather.3.cloned.1.call-update) | async-done | bytes 1048592 | tf_op jit(solution)/shard_map/all_gather | solution.py:32
  334.1 3.4 gather_fusion.1
  337.5 4.4 convolution_bitcast_fusion.2
  341.9 5.6 copy.30
  347.6 8.8 %scatter_fusion.1 = f32[16,128,128]{2,1,0:T(8,128)S(1)} fusion(f32[16,128,128]{2,1,0:T(8,128)S(1)} %broadcast.20.clone, s32[64]{0:T(128)S(1)} %copy-done.6, f32[64,128,128]{2,1,0:T(8,128)} %copy.30), kind=kCustom, calls=%fused_computation.5 | custom fusion | flops 1048576 | bytes 12583168 | tf_op jit(solution)/shard_map/scatter-add | solution.py:17
  356.4 1.0 copy-done.2
  357.5 66.3 %all-reduce.3.cloned.1.call-done = f32[2048,128]{1,0:T(8,128)} async-done(((f32[2048,128]{1,0:T(8,128)}), f32[2048,128]{1,0:T(8,128)}) %all-reduce.3.cloned.1.call-update) | async-done | bytes 1048592 | tf_op jit(solution)/shard_map/psum | solution.py:39
  423.8 2.1 add_convert_fusion
  425.9 2.2 gather_fusion.2
  428.0 5.2 convolution_bitcast_fusion.1
  433.2 5.6 copy.32
  438.8 1.6 broadcast.21
  440.4 13.5 %scatter_fusion.2 = f32[32,128,128]{2,1,0:T(8,128)} fusion(f32[32,128,128]{2,1,0:T(8,128)} %broadcast.21, s32[64]{0:T(128)S(1)} %copy-done.3, f32[64,128,128]{2,1,0:T(8,128)} %copy.32), kind=kCustom, calls=%fused_computation.6 | custom fusion | flops 1048576 | bytes 12583168 | tf_op jit(solution)/shard_map/scatter-add | solution.py:29
  454.0 214.7 %reduce-scatter.5.cloned.1.call-done = f32[1,128,128]{2,1,0:T(8,128)} async-done(((f32[32,128,128]{2,1,0:T(8,128)}), f32[1,128,128]{2,1,0:T(8,128)}) %reduce-scatter.5.cloned.1.call-update) | async-done | bytes 65552 | tf_op jit(solution)/shard_map/reduce_scatter | solution.py:30
  668.7 1.6 fusion
  670.5 75.5 %all-gather.5.cloned.1.call-done = bf16[32,128,128]{2,1,0:T(8,128)(2,1)} async-done(((bf16[1,128,128]{2,1,0:T(8,128)(2,1)}), bf16[32,128,128]{2,1,0:T(8,128)(2,1)}) %all-gather.5.cloned.1.call-update) | async-done | bytes 1048592 | tf_op jit(solution)/shard_map/all_gather | solution.py:32
  746.0 3.4 gather_fusion.3
  749.4 4.4 convolution_bitcast_fusion
  753.8 5.6 copy.34
  759.5 8.8 %scatter_fusion.3 = f32[16,128,128]{2,1,0:T(8,128)S(1)} fusion(f32[16,128,128]{2,1,0:T(8,128)S(1)} %broadcast.20, s32[64]{0:T(128)S(1)} %copy-done.6, f32[64,128,128]{2,1,0:T(8,128)} %copy.34), kind=kCustom, calls=%fused_computation.7 | custom fusion | flops 1048576 | bytes 12583168 | tf_op jit(solution)/shard_map/scatter-add | solution.py:17
  768.3 1.0 copy-done.1
  769.3 66.3 %all-reduce.5.cloned.1.call-done = f32[2048,128]{1,0:T(8,128)} async-done(((f32[2048,128]{1,0:T(8,128)}), f32[2048,128]{1,0:T(8,128)}) %all-reduce.5.cloned.1.call-update) | async-done | bytes 1048592 | tf_op jit(solution)/shard_map/psum | solution.py:39
  835.6 3.3 multiply_add_fusion
  (29 shorter events, 0.8 us)
Async XLA Ops:
  7.2 4.7 copy-start
  7.2 249.2 %reduce-scatter.3.cloned.1.call-start = ((), (), s32[]{:S(2)}) async-start(), calls=%async_computation.2 | async-start | bytes 2162688 | tf_op jit(solution)/shard_map/reduce_scatter | solution.py:30
  22.6 1.6 copy-start.3
  37.7 218.6 %copy-start.4 = (f32[1,128]{1,0:T(1,128)S(1)}, f32[1,128]{1,0:T(1,128)}, u32[]{:S(2)}) copy-start(f32[1,128]{1,0:T(1,128)} %param.12) | copy-start | bytes 1540
  37.7 218.6 %copy-start.5 = (f32[1,128]{1,0:T(1,128)S(1)}, f32[1,128]{1,0:T(1,128)}, u32[]{:S(2)}) copy-start(f32[1,128]{1,0:T(1,128)} %param.13) | copy-start | bytes 1540
  37.7 296.4 %all-gather.3.cloned.1.call-start = ((), (), s32[]{:S(2)}) async-start(), calls=%async_computation.3 | async-start | bytes 1081344 | tf_op jit(solution)/shard_map/all_gather | solution.py:32
  257.9 165.8 %all-reduce.3.cloned.1.call-start = ((), (), s32[]{:S(2)}) async-start(), calls=%async_computation.4 | async-start | bytes 2097152 | tf_op jit(solution)/shard_map/psum | solution.py:39
  341.9 5.7 copy-start.6
  356.4 1.0 copy-start.2
  357.4 311.3 %reduce-scatter.5.cloned.1.call-start = ((), (), s32[]{:S(2)}) async-start(), calls=%async_computation.5 | async-start | bytes 2162688 | tf_op jit(solution)/shard_map/reduce_scatter | solution.py:30
  453.9 292.1 %all-gather.5.cloned.1.call-start = ((), (), s32[]{:S(2)}) async-start(), calls=%async_computation.6 | async-start | bytes 1081344 | tf_op jit(solution)/shard_map/all_gather | solution.py:32
  670.3 165.3 %all-reduce.5.cloned.1.call-start = ((), (), s32[]{:S(2)}) async-start(), calls=%async_computation.7 | async-start | bytes 2097152 | tf_op jit(solution)/shard_map/psum | solution.py:39
  768.3 1.0 copy-start.1
Sparse Core Ops, SparseCore 0:
  37.9 218.4 reduce-scatter.2
  259.9 74.2 all-gather.2
  357.5 66.1 all-reduce.2
  454.0 214.5 reduce-scatter.4
  671.7 74.3 all-gather.4
  769.4 66.1 all-reduce.4
where the time goes:
time: 847 us; the launch traced here: 846 us
  waiting for transfers between devices  718 us (85%)
  other arithmetic  55.7 us (7%)
  local copies, waits for them, and re-layouts  38.7 us (5%)
  matrix products  19.1 us (2%)
  between operations  14.2 us (2%)
    reduce_scatter x2, waiting for transfers between devices, residual_pass(): lax.psum_scatter(partial_value, 'band', scatter_dimension=0, tiled=True)  433 us
    all_gather x2, waiting for transfers between devices, residual_pass(): lax.all_gather(resid.astype(jnp.bfloat16), 'band', axis=0, tiled=True)  152 us
    psum x2, waiting for transfers between devices, summed_grad(): return lax.psum(part, 'shot')  133 us
    scatter-add x2, other arithmetic, residual_pass(): partial_value = jax.ops.segment_sum(prod, bundle_of, num_segments=bundles)  27 us
    scatter-add x2, other arithmetic, adjoint_part(): jax.ops.segment_sum(contrib, cellblock_of, num_segments=cell_blocks)  17.6 us
  transfers between devices with their start and end apart: 6, of which 6 were waited for; matrix products, arithmetic and copies ran while one was open for 0% of the time, Pallas kernels for 0%

commit v1 on v0

--- a/solution.py
+++ b/solution.py
@@ -29,7 +29,12 @@
         partial_value = jax.ops.segment_sum(prod, bundle_of, num_segments=bundles)
         pred = lax.psum_scatter(partial_value, "band", scatter_dimension=0, tiled=True)
         resid = pick_weight[:, :, None] * (pred - observed[:, :, None])
-        resid_all = lax.all_gather(resid.astype(jnp.bfloat16), "band", axis=0, tiled=True)
+        array = resid.astype(jnp.bfloat16)
+        size = lax.axis_size("band")
+        repeats = [size if d == 0 else 1 for d in range(array.ndim)]
+        resid_all = lax.all_to_all(
+            jnp.tile(array, repeats), "band", split_axis=0, concat_axis=0, tiled=True
+        )
         return (resid, adjoint_part(sensitivity, bundle_of, cellblock_of, resid_all, cell_blocks))
 
     probe1 = (state + 0.5 * prior_velocity).astype(jnp.bfloat16)

time: 847 us -> 751 us (0.89)
  waiting for transfers between devices: 718 us -> 586 us
  blocking collectives: 0 us -> 28.7 us
    all_gather x2 -> x0, waiting for transfers between devices: 152 us -> none  [residual_pass(): lax.all_gather(resid.astype(jnp.bfloat16), 'band', axis=0, tiled=True)]
    all_to_all x0 -> x1, blocking collectives: none -> 28.7 us  [residual_pass(): lax.all_to_all(jnp.tile(array, repeats), 'band', split_axis=0, concat_axi...]
    all_to_all x0 -> x1, waiting for transfers between devices: none -> 20.8 us  [residual_pass(): lax.all_to_all(jnp.tile(array, repeats), 'band', split_axis=0, concat_axi...]
  transfers between devices with their start and end apart: 6 -> 5, of which waited for: 6 -> 5; matrix products, arithmetic and copies ran while one was open for 0% -> 0% of each run, Pallas kernels for 0% -> 0%
where the time goes in v1:
time: 751 us; the launch traced here: 749 us
  waiting for transfers between devices  586 us (78%)
  other arithmetic  55.1 us (7%)
  local copies, waits for them, and re-layouts  37.7 us (5%)
  blocking collectives  28.7 us (4%)
  matrix products  19.1 us (3%)
  between operations  13.9 us (2%)
  starting transfers between devices  8.2 us (1%)
    reduce_scatter x2, waiting for transfers between devices, residual_pass(): lax.psum_scatter(partial_value, 'band', scatter_dimension=0, tiled=True)  433 us
    psum x2, waiting for transfers between devices, summed_grad(): return lax.psum(part, 'shot')  133 us
    all_to_all x1, blocking collectives, residual_pass(): lax.all_to_all(jnp.tile(array, repeats), 'band', split_axis=0, concat_axi...  28.7 us
    scatter-add x2, other arithmetic, residual_pass(): partial_value = jax.ops.segment_sum(prod, bundle_of, num_segments=bundles)  27.1 us
    all_to_all x1, waiting for transfers between devices, residual_pass(): lax.all_to_all(jnp.tile(array, repeats), 'band', split_axis=0, concat_axi...  20.8 us
    scatter-add x2, other arithmetic, adjoint_part(): jax.ops.segment_sum(contrib, cellblock_of, num_segments=cell_blocks)  17.6 us
  transfers between devices with their start and end apart: 5, of which 5 were waited for; matrix products, arithmetic and copies ran while one was open for 0% of the time, Pallas kernels for 0%

profile of v1, /device:TPU:2, one launch (start us, length us, event | category | flops | bytes accessed | tf_op | source)
XLA Modules:
  0.0 749.1 jit_solution(2963647071339239053)
XLA Ops:
  8.0 1.7 add_convert_fusion.1
  9.7 2.2 gather_fusion
  11.9 5.2 convolution_bitcast_fusion.3
  17.0 5.6 copy.14
  22.6 1.6 broadcast.25.clone
  24.2 13.5 %scatter_fusion = f32[32,128,128]{2,1,0:T(8,128)} fusion(f32[32,128,128]{2,1,0:T(8,128)} %broadcast.25.clone, s32[64]{0:T(128)S(1)} %copy-done.3, f32[64,128,128]{2,1,0:T(8,128)} %copy.14), kind=kCustom, calls=%fused_computation.4 | custom fusion | flops 1048576 | bytes 12583168 | tf_op jit(solution)/shard_map/scatter-add | solution.py:29
  37.8 218.0 %reduce-scatter.3.cloned.1.call-done = f32[1,128,128]{2,1,0:T(8,128)} async-done(((f32[32,128,128]{2,1,0:T(8,128)}), f32[1,128,128]{2,1,0:T(8,128)}) %reduce-scatter.3.cloned.1.call-update) | async-done | bytes 65552 | tf_op jit(solution)/shard_map/reduce_scatter | solution.py:30
  256.7 1.2 tile.9
  257.9 8.0 %all-to-all-start = ((bf16[32,128,128]{2,1,0:T(8,128)(2,1)}), bf16[32,128,128]{2,1,0:T(8,128)(2,1)S(1)}, u32[]{:S(2)}, u32[]{:S(2)}) async-start(bf16[32,128,128]{2,1,0:T(8,128)(2,1)} %tile.9), calls=%async_computation.1 | async-start | bytes 2097152 | tf_op jit(solution)/shard_map/all_to_all | solution.py:35
  266.1 20.8 %all-to-all-done = bf16[32,128,128]{2,1,0:T(8,128)(2,1)S(1)} async-done(((bf16[32,128,128]{2,1,0:T(8,128)(2,1)}), bf16[32,128,128]{2,1,0:T(8,128)(2,1)S(1)}, u32[]{:S(2)}, u32[]{:S(2)}) %all-to-all-start) | async-done | bytes 1048608 | tf_op jit(solution)/shard_map/all_to_all | solution.py:35
  286.9 2.1 gather_fusion.1
  289.0 4.4 convolution_bitcast_fusion.2
  293.4 5.6 copy.16
  299.1 8.8 %scatter_fusion.1 = f32[16,128,128]{2,1,0:T(8,128)S(1)} fusion(f32[16,128,128]{2,1,0:T(8,128)S(1)} %broadcast.24.clone, s32[64]{0:T(128)S(1)} %copy-done.6, f32[64,128,128]{2,1,0:T(8,128)} %copy.16), kind=kCustom, calls=%fused_computation.5 | custom fusion | flops 1048576 | bytes 12583168 | tf_op jit(solution)/shard_map/scatter-add | solution.py:17
  308.0 1.0 copy-done.2
  309.0 66.4 %all-reduce.3.cloned.1.call-done = f32[2048,128]{1,0:T(8,128)} async-done(((f32[2048,128]{1,0:T(8,128)}), f32[2048,128]{1,0:T(8,128)}) %all-reduce.3.cloned.1.call-update) | async-done | bytes 1048592 | tf_op jit(solution)/shard_map/psum | solution.py:44
  375.4 2.1 add_convert_fusion
  377.5 2.2 gather_fusion.2
  379.7 5.2 convolution_bitcast_fusion.1
  384.9 5.6 copy.18
  390.5 1.6 broadcast.25
  392.1 13.5 %scatter_fusion.2 = f32[32,128,128]{2,1,0:T(8,128)} fusion(f32[32,128,128]{2,1,0:T(8,128)} %broadcast.25, s32[64]{0:T(128)S(1)} %copy-done.3, f32[64,128,128]{2,1,0:T(8,128)} %copy.18), kind=kCustom, calls=%fused_computation.6 | custom fusion | flops 1048576 | bytes 12583168 | tf_op jit(solution)/shard_map/scatter-add | solution.py:29
  405.7 214.6 %reduce-scatter.5.cloned.1.call-done = f32[1,128,128]{2,1,0:T(8,128)} async-done(((f32[32,128,128]{2,1,0:T(8,128)}), f32[1,128,128]{2,1,0:T(8,128)}) %reduce-scatter.5.cloned.1.call-update) | async-done | bytes 65552 | tf_op jit(solution)/shard_map/reduce_scatter | solution.py:30
  620.3 1.6 convert_bitcast_fusion
  622.1 28.7 %all_to_all.10 = bf16[32,128,128]{2,1,0:T(8,128)(2,1)S(1)} all-to-all(bf16[32,128,128]{2,1,0:T(8,128)(2,1)S(1)} %tile.21), channel_id=1, replica_groups=mesh['shot'=8,'band'=32] {'band'}, dimensions={0} | all-to-all | bytes 2097152 | tf_op jit(solution)/shard_map/all_to_all | solution.py:35
  650.8 2.1 gather_fusion.3
  652.9 4.4 convolution_bitcast_fusion
  657.3 5.6 copy.20
  663.0 8.8 %scatter_fusion.3 = f32[16,128,128]{2,1,0:T(8,128)S(1)} fusion(f32[16,128,128]{2,1,0:T(8,128)S(1)} %broadcast.24, s32[64]{0:T(128)S(1)} %copy-done.6, f32[64,128,128]{2,1,0:T(8,128)} %copy.20), kind=kCustom, calls=%fused_computation.7 | custom fusion | flops 1048576 | bytes 12583168 | tf_op jit(solution)/shard_map/scatter-add | solution.py:17
  671.8 1.0 copy-done.1
  672.8 66.5 %all-reduce.5.cloned.1.call-done = f32[2048,128]{1,0:T(8,128)} async-done(((f32[2048,128]{1,0:T(8,128)}), f32[2048,128]{1,0:T(8,128)}) %all-reduce.5.cloned.1.call-update) | async-done | bytes 1048592 | tf_op jit(solution)/shard_map/psum | solution.py:44
  739.3 3.3 multiply_add_fusion
  (28 shorter events, 2.4 us)
Async XLA Ops:
  7.2 4.7 copy-start
  7.2 248.6 %reduce-scatter.3.cloned.1.call-start = ((), (), s32[]{:S(2)}) async-start(), calls=%async_computation.4 | async-start | bytes 2162688 | tf_op jit(solution)/shard_map/reduce_scatter | solution.py:30
  22.6 1.6 copy-start.3
  37.7 218.0 %copy-start.4 = (f32[1,128]{1,0:T(1,128)S(1)}, f32[1,128]{1,0:T(1,128)}, u32[]{:S(2)}) copy-start(f32[1,128]{1,0:T(1,128)} %param.12) | copy-start | bytes 1540
  37.8 218.0 %copy-start.5 = (f32[1,128]{1,0:T(1,128)S(1)}, f32[1,128]{1,0:T(1,128)}, u32[]{:S(2)}) copy-start(f32[1,128]{1,0:T(1,128)} %param.13) | copy-start | bytes 1540
  257.9 29.0 %all-to-all-start = ((bf16[32,128,128]{2,1,0:T(8,128)(2,1)}), bf16[32,128,128]{2,1,0:T(8,128)(2,1)S(1)}, u32[]{:S(2)}, u32[]{:S(2)}) async-start(bf16[32,128,128]{2,1,0:T(8,128)(2,1)} %tile.9), calls=%async_computation.1 | async-start | bytes 2097152 | tf_op jit(solution)/shard_map/all_to_all | solution.py:35
  266.0 109.5 %all-reduce.3.cloned.1.call-start = ((), (), s32[]{:S(2)}) async-start(), calls=%async_computation.5 | async-start | bytes 2097152 | tf_op jit(solution)/shard_map/psum | solution.py:44
  293.4 5.7 copy-start.6
  307.9 1.0 copy-start.2
  308.9 311.3 %reduce-scatter.5.cloned.1.call-start = ((), (), s32[]{:S(2)}) async-start(), calls=%async_computation.6 | async-start | bytes 2162688 | tf_op jit(solution)/shard_map/reduce_scatter | solution.py:30
  405.6 333.6 %all-reduce.5.cloned.1.call-start = ((), (), s32[]{:S(2)}) async-start(), calls=%async_computation.7 | async-start | bytes 2097152 | tf_op jit(solution)/shard_map/psum | solution.py:44
  671.8 1.0 copy-start.1
Sparse Core Ops, SparseCore 0:
  37.9 217.8 reduce-scatter.2
  309.1 66.3 all-reduce.2
  405.7 214.4 reduce-scatter.4
  672.9 66.2 all-reduce.4
